TPU v7x, 32 devices: a whole 2x2x4 slice. The times are simulated.
32 devices in a mesh: row: 8 (over z, y), col: 4 (over x, core).
Axes of the slice: x: 2, y: 2, z: 4, core: 2. Of those that a mesh axis runs over, the one named last changes fastest.
Arguments:
- s_rows: bfloat16 [8192, 256], P('row', 'col'), may hold values from -0.375 to 0.375
- iterate: bfloat16 [256, 32768], P('row', 'col'), may hold values from -6 to 6
Outputs:
- product: bfloat16 [8192, 32768], P('row', 'col')
All inputs are finite; a program needn't handle non-finite values.
Results may differ from a plain program's by a relative error of at most 0.001.
Values may be sent and summed in bfloat16 or wider, within the bound.
A program may use at most 64 MiB of HBM per device.

v0:
```python
import jax
import jax.numpy as jnp
from jax import lax
from jax.sharding import PartitionSpec as P


def shards(s_rows, iterate):
    panel_rows = lax.all_gather(s_rows, "col", axis=1, tiled=True)
    whole = lax.all_gather(iterate, "row", axis=0, tiled=True)
    product = jnp.dot(panel_rows, whole, preferred_element_type=jnp.float32)
    return product.astype(jnp.bfloat16)


def solution(mesh):
    return jax.shard_map(
        shards,
        mesh=mesh,
        in_specs=(P("row", "col"), P("row", "col")),
        out_specs=P("row", "col"),
        check_vma=False,
    )
```

profile of v0, /device:TPU:0, one launch (start us, length us, event | category | flops | bytes accessed | tf_op | source)
XLA Modules:
  0.0 103.2 jit_solution(14347596570096783215)
XLA Ops:
  6.5 0.0 all-gather.2.cloned.1.call-start
  6.5 0.7 all-gather.2.cloned.1.call-update
  7.3 8.8 %all_gather.6 = bf16[1024,256]{0,1:T(8,128)(2,1)S(1)} all-gather(bf16[1024,64]{0,1:T(8,128)(2,1)} %param.2), channel_id=1, replica_groups=mesh['row'=8,'col'=4] {'col'}, dimensions={1}, use_global_device_ids=true | all-gather | bytes 655360 | tf_op jit(solution)/shard_map/all_gather | solution.py:8
  16.1 69.5 %all-gather.2.cloned.1.call-done = bf16[256,8192]{1,0:T(8,128)(2,1)} async-done(((bf16[32,8192]{1,0:T(8,128)(2,1)}), bf16[256,8192]{1,0:T(8,128)(2,1)}) %all-gather.2.cloned.1.call-update) | async-done | bytes 4194320 | tf_op jit(solution)/shard_map/all_gather | solution.py:9
  85.6 10.7 %convolution_convert_fusion = bf16[1024,8192]{1,0:T(8,128)(2,1)} fusion(bf16[1024,256]{0,1:T(8,128)(2,1)S(1)} %all_gather.6, bf16[256,8192]{1,0:T(8,128)(2,1)} %all-gather.2.cloned.1.call-done), kind=kOutput, calls=%fused_computation | convolution fusion | flops 4303355904 | bytes 21495808 | tf_op jit(solution)/shard_map/dot_general | solution.py:10
Async XLA Ops:
  6.5 79.1 %all-gather.2.cloned.1.call-start = ((), (), s32[]{:S(2)}) async-start(), calls=%async_computation | async-start | bytes 4718592 | tf_op jit(solution)/shard_map/all_gather | solution.py:9
Sparse Core Ops, SparseCore 0:
  9.5 76.0 all-gather.1
where the time goes:
time: 103 us
  waiting for transfers between devices  70.2 us (68%)
  between operations  13.4 us (13%)
  matrix products  10.7 us (10%)
  blocking collectives  8.83 us (9%)
    all_gather x1, waiting for transfers between devices, shards(): whole = lax.all_gather(iterate, 'row', axis=0, tiled=True)  69.5 us
    dot_general x1, matrix products, shards(): product = jnp.dot(panel_rows, whole, preferred_element_type=jnp.float32)  10.7 us
    all_gather x1, blocking collectives, shards(): panel_rows = lax.all_gather(s_rows, 'col', axis=1, tiled=True)  8.83 us
  transfers between devices with their start and end apart: 1, of which 1 were waited for; matrix products, arithmetic and copies ran while one was open for 0% of the time, Pallas kernels for 0%

commit v1 on v0

v1 whole, which is shorter than its diff:
```python
import functools

import jax
import jax.numpy as jnp
from jax import lax
from jax.experimental import pallas as pl
from jax.experimental.pallas import tpu as pltpu
from jax.sharding import PartitionSpec as P

MESH = pl.DeviceIdType.MESH
CHUNKS = 8
LINE = 4
TILE = 1024


def gather_kernel(st_ref, it_ref, s_ref, whole_ref, st_all, zsend, ysend, xsend, recv, s_send, s_recv, local):
    row, col = lax.axis_index("row"), lax.axis_index("col")
    z, y = row // 2, row % 2
    other = row + 1 - 2 * y
    pair = z + 1 - 2 * (z % 2)
    depth, columns = it_ref.shape
    width = columns // CHUNKS
    half = CHUNKS // 2
    kdepth = st_ref.shape[0]
    below, above = z > 0, z < LINE - 1

    def block(zz, yy, c):
        return (
            pl.ds(pl.multiple_of((2 * zz + yy) * depth, depth), depth),
            pl.ds(pl.multiple_of(c * width, width), width),
        )

    def own(c):
        return it_ref.at[:, pl.ds(pl.multiple_of(c * width, width), width)]

    def send(src, zz, yy, c, sem, target):
        return pltpu.make_async_remote_copy(
            src_ref=src,
            dst_ref=whole_ref.at[block(zz, yy, c)],
            send_sem=sem,
            recv_sem=recv.at[2 * zz + yy, c],
            device_id={"row": target},
            device_id_type=MESH,
        )

    def held(zz, yy, c):
        return whole_ref.at[block(zz, yy, c)]

    def down(src, zz, c):
        return send(src, zz, y, c, zsend.at[0, zz, c], row - 2)

    def up(src, zz, c):
        return send(src, zz, y, c, zsend.at[1, zz, c], row + 2)

    def across(src, zz, c):
        return send(src, zz, y, c, ysend.at[zz, c], other)

    def extra(c):
        return send(held(z, 1 - y, c), z, 1 - y, c, xsend.at[c], 2 * pair + y)

    def s_copy(k):
        far = (col // 2 + k // 2) % 2 * 2 + (col + k) % 2
        at = pl.ds(pl.multiple_of(col * kdepth, kdepth), kdepth)
        return pltpu.make_async_remote_copy(
            src_ref=st_ref,
            dst_ref=st_all.at[at],
            send_sem=s_send.at[k - 1],
            recv_sem=s_recv.at[k - 1],
            device_id={"col": far},
            device_id_type=MESH,
        )

    def arrived(zz, yy, c):
        pltpu.make_async_copy(held(zz, yy, c), held(zz, yy, c), recv.at[2 * zz + yy, c]).wait()

    mine = pltpu.make_async_copy(it_ref, whole_ref.at[pl.ds(pl.multiple_of(row * depth, depth), depth)], local.at[0])
    mine.start()
    mine_s = pltpu.make_async_copy(st_ref, st_all.at[pl.ds(pl.multiple_of(col * kdepth, kdepth), kdepth)], local.at[1])
    mine_s.start()

    barrier = pltpu.get_barrier_semaphore()

    @pl.when(below)
    def _():
        pl.semaphore_signal(barrier, inc=1, device_id={"row": row - 2}, device_id_type=MESH)

    @pl.when(above)
    def _():
        pl.semaphore_signal(barrier, inc=1, device_id={"row": row + 2}, device_id_type=MESH)

    pl.semaphore_signal(barrier, inc=1, device_id={"row": other}, device_id_type=MESH)
    for k in range(1, 4):
        far = (col // 2 + k // 2) % 2 * 2 + (col + k) % 2
        pl.semaphore_signal(barrier, inc=1, device_id={"col": far}, device_id_type=MESH)
    pl.semaphore_wait(barrier, 4 + below.astype(jnp.int32) + above.astype(jnp.int32))

    @pl.loop(0, CHUNKS)
    def _(c):
        @pl.when(below)
        def _():
            down(own(c), z, c).start()

        @pl.when(above)
        def _():
            up(own(c), z, c).start()

        across(own(c), z, c).start()

    for k in range(1, 4):
        s_copy(k).start()

    def pass_on(d):
        @pl.loop(0, CHUNKS)
        def _(c):
            for sign in (1, -1):
                zz = z + sign * d

                @pl.when((zz >= 0) & (zz < LINE))
                def _():
                    arrived(zz, y, c)
                    src = held(zz, y, c)

                    @pl.when(below if sign == 1 else above)
                    def _():
                        (down if sign == 1 else up)(src, zz, c).start()

                    @pl.when((zz != pair) | (c < half))
                    def _():
                        across(src, zz, c).start()

    pass_on(1)
    for k in range(1, 4):
        s_copy(k).wait_recv()
    mine_s.wait()
    s_ref[...] = st_all[...].T
    pass_on(2)

    @pl.loop(half, CHUNKS)
    def _(c):
        arrived(z, 1 - y, c)
        extra(c).start()

    pass_on(3)

    @pl.loop(0, CHUNKS)
    def _(c):
        for zz in range(LINE):
            @pl.when((zz != z) | (c < half))
            def _():
                arrived(zz, 1 - y, c)

    @pl.loop(0, CHUNKS)
    def _(c):
        for zz in range(LINE):
            @pl.when(below & (zz >= z))
            def _():
                down(own(c), zz, c).wait_send()

            @pl.when(above & (zz <= z))
            def _():
                up(own(c), zz, c).wait_send()

            @pl.when((zz != pair) | (c < half))
            def _():
                across(own(c), zz, c).wait_send()

        @pl.when(c >= half)
        def _():
            extra(c).wait_send()

    for k in range(1, 4):
        s_copy(k).wait_send()
    mine.wait()


def product_kernel(s_ref, w_ref, o_ref):
    o_ref[...] = jnp.dot(s_ref[...], w_ref[...], preferred_element_type=jnp.float32).astype(o_ref.dtype)


def gathered(s_rows, iterate):
    rows, part = s_rows.shape
    depth, columns = iterate.shape
    blocks = 2 * LINE
    dma = pltpu.SemaphoreType.DMA
    s, whole = pl.pallas_call(
        gather_kernel,
        out_shape=(
            jax.ShapeDtypeStruct((rows, 4 * part), s_rows.dtype),
            jax.ShapeDtypeStruct((blocks * depth, columns), iterate.dtype),
        ),
        in_specs=[pl.BlockSpec(memory_space=pl.ANY)] * 2,
        out_specs=(pl.BlockSpec(memory_space=pltpu.VMEM), pl.BlockSpec(memory_space=pl.ANY)),
        scratch_shapes=[
            pltpu.VMEM((4 * part, rows), s_rows.dtype),
            dma((2, LINE, CHUNKS)),
            dma((LINE, CHUNKS)),
            dma((CHUNKS,)),
            dma((blocks, CHUNKS)),
            dma((3,)),
            dma((3,)),
            dma((2,)),
        ],
        compiler_params=pltpu.CompilerParams(collective_id=0, has_side_effects=True),
    )(s_rows.T, iterate)
    return pl.pallas_call(
        product_kernel,
        grid=(columns // TILE,),
        in_specs=[
            pl.BlockSpec(s.shape, lambda j: (0, 0)),
            pl.BlockSpec((whole.shape[0], TILE), lambda j: (0, j)),
        ],
        out_specs=pl.BlockSpec((rows, TILE), lambda j: (0, j)),
        out_shape=jax.ShapeDtypeStruct((rows, columns), jnp.bfloat16),
        compiler_params=pltpu.CompilerParams(vmem_limit_bytes=60 << 20),
    )(s, whole)


def shards(s_rows, iterate):
    panel_rows = lax.all_gather(s_rows, "col", axis=1, tiled=True)
    whole = lax.all_gather(iterate, "row", axis=0, tiled=True)
    product = jnp.dot(panel_rows, whole, preferred_element_type=jnp.float32)
    return product.astype(jnp.bfloat16)


def solution(mesh):
    small = mesh.shape["row"] == 2 * LINE and mesh.shape["col"] == 4
    return jax.shard_map(
        gathered if small else shards,
        mesh=mesh,
        in_specs=(P("row", "col"), P("row", "col")),
        out_specs=P("row", "col"),
        check_vma=False,
    )
```

time: 103 us -> 59.1 us (0.57)
  waiting for transfers between devices: 70.2 us -> 0 us
  Pallas kernels: 0 us -> 58.8 us
  between operations: 13.4 us -> 0.01 us
  matrix products: 10.7 us -> 0 us
  blocking collectives: 8.83 us -> 0 us
    all_gather x1 -> x0, waiting for transfers between devices: 69.5 us -> none  [shards(): whole = lax.all_gather(iterate, 'row', axis=0, tiled=True)]
    pallas_call x0 -> x2, Pallas kernels: none -> 58.8 us  [the longest x1 47.7 us: gathered(): pl.pallas_call(gather_kernel, out_shape=(jax.ShapeDtypeStruct((rows, 4 *...]
    dot_general x1 -> x0, matrix products: 10.7 us -> none  [shards(): product = jnp.dot(panel_rows, whole, preferred_element_type=jnp.float32)]
    all_gather x1 -> x0, blocking collectives: 8.83 us -> none  [shards(): panel_rows = lax.all_gather(s_rows, 'col', axis=1, tiled=True)]
  transfers between devices with their start and end apart: 1 -> 0, of which waited for: 1 -> 0; matrix products, arithmetic and copies ran while one was open for 0% -> 0% of each run, Pallas kernels for 0% -> 0%
where the time goes in v1:
time: 59.1 us; the launch traced here: 58.8 us
  Pallas kernels  58.8 us (99%)
    pallas_call x1, Pallas kernels, gathered(): pl.pallas_call(gather_kernel, out_shape=(jax.ShapeDtypeStruct((rows, 4 *...  47.7 us
    pallas_call x1, Pallas kernels, gathered(): pl.pallas_call(product_kernel, grid=(columns // TILE,), in_specs=[pl.Bloc...  11.1 us

profile of v1, /device:TPU:0, one launch (start us, length us, event | category | flops | bytes accessed | tf_op | source)
XLA Modules:
  0.0 58.8 jit_solution(14368364633644019383)
XLA Ops:
  0.0 47.7 %shard_map.28 = (bf16[1024,256]{1,0:T(8,128)(2,1)}, bf16[256,8192]{1,0:T(8,128)(2,1)}) custom-call(bf16[64,1024]{1,0:T(8,128)(2,1)} %bitcast.1, bf16[32,8192]{1,0:T(8,128)(2,1)} %it_ref.1), custom_call_target="tpu_custom_call" | custom-call | tf_op jit(solution)/shard_map/pallas_call | solution.py:185
  47.7 11.1 %shard_map.29 = bf16[1024,8192]{1,0:T(8,128)(2,1)} custom-call(bf16[1024,256]{1,0:T(8,128)(2,1)} %get-tuple-element.7.s_ref, bf16[256,8192]{1,0:T(8,128)(2,1)} %get-tuple-element.8.w_ref), custom_call_target="tpu_custom_call" | custom-call | tf_op jit(solution)/shard_map/pallas_call | solution.py:205

commit v2 on v1

--- a/solution.py
+++ b/solution.py
@@ -10,10 +10,10 @@
 MESH = pl.DeviceIdType.MESH
 CHUNKS = 8
 LINE = 4
-TILE = 1024
-
-
-def gather_kernel(st_ref, it_ref, s_ref, whole_ref, st_all, zsend, ysend, xsend, recv, s_send, s_recv, local):
+LAG = 4
+
+
+def gather_kernel(st_ref, it_ref, o_ref, whole_ref, s, st_all, zsend, ysend, xsend, recv, s_send, s_recv, local):
     row, col = lax.axis_index("row"), lax.axis_index("col")
     z, y = row // 2, row % 2
     other = row + 1 - 2 * y
@@ -108,46 +108,57 @@
 
     for k in range(1, 4):
         s_copy(k).start()
-
-    def pass_on(d):
-        @pl.loop(0, CHUNKS)
-        def _(c):
-            for sign in (1, -1):
-                zz = z + sign * d
-
-                @pl.when((zz >= 0) & (zz < LINE))
-                def _():
-                    arrived(zz, y, c)
-                    src = held(zz, y, c)
-
-                    @pl.when(below if sign == 1 else above)
-                    def _():
-                        (down if sign == 1 else up)(src, zz, c).start()
-
-                    @pl.when((zz != pair) | (c < half))
-                    def _():
-                        across(src, zz, c).start()
-
-    pass_on(1)
     for k in range(1, 4):
         s_copy(k).wait_recv()
     mine_s.wait()
-    s_ref[...] = st_all[...].T
-    pass_on(2)
-
-    @pl.loop(half, CHUNKS)
-    def _(c):
-        arrived(z, 1 - y, c)
-        extra(c).start()
-
-    pass_on(3)
-
-    @pl.loop(0, CHUNKS)
-    def _(c):
+    s[...] = st_all[...].T
+    mine.wait()
+
+    def pass_on(d, c):
+        for sign in (1, -1):
+            zz = z + sign * d
+
+            @pl.when((zz >= 0) & (zz < LINE))
+            def _():
+                arrived(zz, y, c)
+                src = held(zz, y, c)
+
+                @pl.when(below if sign == 1 else above)
+                def _():
+                    (down if sign == 1 else up)(src, zz, c).start()
+
+                @pl.when((zz != pair) | (c < half))
+                def _():
+                    across(src, zz, c).start()
+
+    def multiply(c):
         for zz in range(LINE):
             @pl.when((zz != z) | (c < half))
             def _():
                 arrived(zz, 1 - y, c)
+
+        w = whole_ref[:, pl.ds(pl.multiple_of(c * width, width), width)]
+        o_ref[c] = jnp.dot(s[...], w, preferred_element_type=jnp.float32).astype(o_ref.dtype)
+
+    @pl.loop(0, CHUNKS + LAG)
+    def _(t):
+        @pl.when(t < CHUNKS)
+        def _():
+            pass_on(1, t)
+
+        for d in (2, 3):
+            @pl.when((t >= d - 1) & (t < CHUNKS + d - 1))
+            def _():
+                pass_on(d, t - d + 1)
+
+        @pl.when((t >= half + 2) & (t < CHUNKS + 2))
+        def _():
+            arrived(z, 1 - y, t - 2)
+            extra(t - 2).start()
+
+        @pl.when(t >= LAG)
+        def _():
+            multiply(t - LAG)
 
     @pl.loop(0, CHUNKS)
     def _(c):
@@ -170,27 +181,33 @@
 
     for k in range(1, 4):
         s_copy(k).wait_send()
-    mine.wait()
-
-
-def product_kernel(s_ref, w_ref, o_ref):
-    o_ref[...] = jnp.dot(s_ref[...], w_ref[...], preferred_element_type=jnp.float32).astype(o_ref.dtype)
+
+
+def write_kernel(part_ref, out_ref, sems):
+    chunks, _, width = part_ref.shape
+    copies = [
+        pltpu.make_async_copy(part_ref.at[c], out_ref.at[:, c * width : (c + 1) * width], sems.at[c])
+        for c in range(chunks)
+    ]
+    for copy in copies:
+        copy.start()
+    for copy in copies:
+        copy.wait()
 
 
 def gathered(s_rows, iterate):
     rows, part = s_rows.shape
     depth, columns = iterate.shape
-    blocks = 2 * LINE
+    blocks, width = 2 * LINE, columns // CHUNKS
     dma = pltpu.SemaphoreType.DMA
-    s, whole = pl.pallas_call(
+    product = pl.pallas_call(
         gather_kernel,
-        out_shape=(
-            jax.ShapeDtypeStruct((rows, 4 * part), s_rows.dtype),
-            jax.ShapeDtypeStruct((blocks * depth, columns), iterate.dtype),
-        ),
+        out_shape=pltpu.VMEM((CHUNKS, rows, width), jnp.bfloat16),
         in_specs=[pl.BlockSpec(memory_space=pl.ANY)] * 2,
-        out_specs=(pl.BlockSpec(memory_space=pltpu.VMEM), pl.BlockSpec(memory_space=pl.ANY)),
+        out_specs=pl.BlockSpec(memory_space=pltpu.VMEM),
         scratch_shapes=[
+            pltpu.VMEM((blocks * depth, columns), iterate.dtype),
+            pltpu.VMEM((rows, 4 * part), s_rows.dtype),
             pltpu.VMEM((4 * part, rows), s_rows.dtype),
             dma((2, LINE, CHUNKS)),
             dma((LINE, CHUNKS)),
@@ -200,19 +217,16 @@
             dma((3,)),
             dma((2,)),
         ],
-        compiler_params=pltpu.CompilerParams(collective_id=0, has_side_effects=True),
+        compiler_params=pltpu.CompilerParams(collective_id=0, has_side_effects=True, vmem_limit_bytes=44 << 20),
     )(s_rows.T, iterate)
     return pl.pallas_call(
-        product_kernel,
-        grid=(columns // TILE,),
-        in_specs=[
-            pl.BlockSpec(s.shape, lambda j: (0, 0)),
-            pl.BlockSpec((whole.shape[0], TILE), lambda j: (0, j)),
-        ],
-        out_specs=pl.BlockSpec((rows, TILE), lambda j: (0, j)),
+        write_kernel,
+        in_specs=[pl.BlockSpec(memory_space=pltpu.VMEM)],
+        out_specs=pl.BlockSpec(memory_space=pl.ANY),
         out_shape=jax.ShapeDtypeStruct((rows, columns), jnp.bfloat16),
-        compiler_params=pltpu.CompilerParams(vmem_limit_bytes=60 << 20),
-    )(s, whole)
+        scratch_shapes=[dma((CHUNKS,))],
+        compiler_params=pltpu.CompilerParams(vmem_limit_bytes=24 << 20),
+    )(product)
 
 
 def shards(s_rows, iterate):

time: 59.1 us -> 56.5 us (0.956)
  Pallas kernels: 58.8 us -> 56.4 us
    pallas_call x2, Pallas kernels: 58.8 us -> 56.4 us  [the longest x1 50.5 us: gathered(): pl.pallas_call(gather_kernel, out_shape=pltpu.VMEM((CHUNKS, rows, width),...]
where the time goes in v2:
time: 56.5 us; the launch traced here: 56.4 us
  Pallas kernels  56.4 us (100%)
    pallas_call x1, Pallas kernels, gathered(): pl.pallas_call(gather_kernel, out_shape=pltpu.VMEM((CHUNKS, rows, width),...  50.5 us
    pallas_call x1, Pallas kernels, gathered(): pl.pallas_call(write_kernel, in_specs=[pl.BlockSpec(memory_space=pltpu.VM...  5.92 us

profile of v2, /device:TPU:0, one launch (start us, length us, event | category | flops | bytes accessed | tf_op | source)
XLA Modules:
  0.0 56.4 jit_solution(6357639287618734977)
XLA Ops:
  0.0 50.5 %shard_map.28.part_ref = bf16[8,1024,1024]{2,1,0:T(8,128)(2,1)S(1)} custom-call(bf16[64,1024]{1,0:T(8,128)(2,1)} %bitcast.1, bf16[32,8192]{1,0:T(8,128)(2,1)} %it_ref.1), custom_call_target="tpu_custom_call" | custom-call | tf_op jit(solution)/shard_map/pallas_call | solution.py:203
  50.5 5.9 %shard_map.29 = bf16[1024,8192]{1,0:T(8,128)(2,1)} custom-call(bf16[8,1024,1024]{2,1,0:T(8,128)(2,1)S(1)} %shard_map.28.part_ref), custom_call_target="tpu_custom_call" | custom-call | tf_op jit(solution)/shard_map/pallas_call | solution.py:222

commit v3 on v2

--- a/solution.py
+++ b/solution.py
@@ -8,9 +8,11 @@
 from jax.sharding import PartitionSpec as P
 
 MESH = pl.DeviceIdType.MESH
-CHUNKS = 8
+CHUNKS = 4
+HOLD = 1
+TILE = 512
 LINE = 4
-LAG = 4
+LAG = 3
 
 
 def gather_kernel(st_ref, it_ref, o_ref, whole_ref, s, st_all, zsend, ysend, xsend, recv, s_send, s_recv, local):
@@ -137,8 +139,10 @@
             def _():
                 arrived(zz, 1 - y, c)
 
-        w = whole_ref[:, pl.ds(pl.multiple_of(c * width, width), width)]
-        o_ref[c] = jnp.dot(s[...], w, preferred_element_type=jnp.float32).astype(o_ref.dtype)
+        @pl.when(c < CHUNKS - HOLD)
+        def _():
+            w = whole_ref[:, pl.ds(pl.multiple_of(c * width, width), width)]
+            o_ref[c] = jnp.dot(s[...], w, preferred_element_type=jnp.float32).astype(o_ref.dtype)
 
     @pl.loop(0, CHUNKS + LAG)
     def _(t):
@@ -183,16 +187,33 @@
         s_copy(k).wait_send()
 
 
-def write_kernel(part_ref, out_ref, sems):
+def write_kernel(part_ref, whole_ref, s_ref, out_ref, late, sems, late_sems):
     chunks, _, width = part_ref.shape
+    tiles, _, tile = late.shape
     copies = [
         pltpu.make_async_copy(part_ref.at[c], out_ref.at[:, c * width : (c + 1) * width], sems.at[c])
         for c in range(chunks)
     ]
     for copy in copies:
         copy.start()
+
+    def at(t):
+        return pl.ds(pl.multiple_of(chunks * width + t * tile, tile), tile)
+
+    def tail(t):
+        return pltpu.make_async_copy(late.at[t], out_ref.at[:, at(t)], late_sems.at[t])
+
+    @pl.loop(0, tiles)
+    def _(t):
+        late[t] = jnp.dot(s_ref[...], whole_ref[:, at(t)], preferred_element_type=jnp.float32).astype(late.dtype)
+        tail(t).start()
+
     for copy in copies:
         copy.wait()
+
+    @pl.loop(0, tiles)
+    def _(t):
+        tail(t).wait()
 
 
 def gathered(s_rows, iterate):
@@ -200,14 +221,19 @@
     depth, columns = iterate.shape
     blocks, width = 2 * LINE, columns // CHUNKS
     dma = pltpu.SemaphoreType.DMA
-    product = pl.pallas_call(
+    tile = min(TILE, width)
+    tiles = HOLD * width // tile
+    vmem = pl.BlockSpec(memory_space=pltpu.VMEM)
+    part, whole, s = pl.pallas_call(
         gather_kernel,
-        out_shape=pltpu.VMEM((CHUNKS, rows, width), jnp.bfloat16),
-        in_specs=[pl.BlockSpec(memory_space=pl.ANY)] * 2,
-        out_specs=pl.BlockSpec(memory_space=pltpu.VMEM),
-        scratch_shapes=[
+        out_shape=(
+            pltpu.VMEM((CHUNKS - HOLD, rows, width), jnp.bfloat16),
             pltpu.VMEM((blocks * depth, columns), iterate.dtype),
             pltpu.VMEM((rows, 4 * part), s_rows.dtype),
+        ),
+        in_specs=[pl.BlockSpec(memory_space=pl.ANY)] * 2,
+        out_specs=(vmem, vmem, vmem),
+        scratch_shapes=[
             pltpu.VMEM((4 * part, rows), s_rows.dtype),
             dma((2, LINE, CHUNKS)),
             dma((LINE, CHUNKS)),
@@ -217,16 +243,16 @@
             dma((3,)),
             dma((2,)),
         ],
-        compiler_params=pltpu.CompilerParams(collective_id=0, has_side_effects=True, vmem_limit_bytes=44 << 20),
+        compiler_params=pltpu.CompilerParams(collective_id=0, has_side_effects=True, vmem_limit_bytes=16 << 20),
     )(s_rows.T, iterate)
     return pl.pallas_call(
         write_kernel,
-        in_specs=[pl.BlockSpec(memory_space=pltpu.VMEM)],
+        in_specs=[vmem] * 3,
         out_specs=pl.BlockSpec(memory_space=pl.ANY),
         out_shape=jax.ShapeDtypeStruct((rows, columns), jnp.bfloat16),
-        scratch_shapes=[dma((CHUNKS,))],
-        compiler_params=pltpu.CompilerParams(vmem_limit_bytes=24 << 20),
-    )(product)
+        scratch_shapes=[pltpu.VMEM((tiles, rows, tile), jnp.bfloat16), dma((CHUNKS - HOLD,)), dma((tiles,))],
+        compiler_params=pltpu.CompilerParams(vmem_limit_bytes=16 << 20),
+    )(part, whole, s)
 
 
 def shards(s_rows, iterate):

time: 56.5 us -> 54 us (0.956)
  Pallas kernels: 56.4 us -> 51.9 us
  local copies, waits for them, and re-layouts: 0 us -> 1.94 us
    pallas_call x2, Pallas kernels: 56.4 us -> 51.9 us  [the longest x1 46 us: gathered(): pl.pallas_call(gather_kernel, out_shape=(pltpu.VMEM((CHUNKS - HOLD, rows,...]
    unnamed x0 -> x4, local copies, waits for them, and re-layouts: none -> 1.94 us
where the time goes in v3:
time: 54 us; the launch traced here: 53.8 us
  Pallas kernels  51.9 us (96%)
  local copies, waits for them, and re-layouts  1.94 us (4%)
    pallas_call x1, Pallas kernels, gathered(): pl.pallas_call(gather_kernel, out_shape=(pltpu.VMEM((CHUNKS - HOLD, rows,...  46 us
    pallas_call x1, Pallas kernels, gathered(): pl.pallas_call(write_kernel, in_specs=[vmem] * 3, out_specs=pl.BlockSpec(...  5.88 us
    unnamed x4, local copies, waits for them, and re-layouts  1.94 us

profile of v3, /device:TPU:0, one launch (start us, length us, event | category | flops | bytes accessed | tf_op | source)
XLA Modules:
  0.0 53.8 jit_solution(7808222121850835886)
XLA Ops:
  0.0 0.0 copy-start
  0.0 1.0 %copy-done = bf16[32,8192]{1,0:T(8,128)(2,1)S(1)} copy-done((bf16[32,8192]{1,0:T(8,128)(2,1)S(1)}, bf16[32,8192]{1,0:T(8,128)(2,1)}, u32[]{:S(2)}) %copy-start) | copy-done | bytes 524312
  1.0 0.0 copy-start.1
  1.0 0.9 %copy-done.1 = bf16[1024,64]{0,1:T(8,128)(2,1)S(1)} copy-done((bf16[1024,64]{0,1:T(8,128)(2,1)S(1)}, bf16[1024,64]{0,1:T(8,128)(2,1)}, u32[]{:S(2)}) %copy-start.1) | copy-done | bytes 131096
  1.9 46.0 %shard_map.28 = (bf16[3,1024,2048]{2,1,0:T(8,128)(2,1)S(1)}, bf16[256,8192]{1,0:T(8,128)(2,1)S(1)}, bf16[1024,256]{1,0:T(8,128)(2,1)S(1)}) custom-call(bf16[64,1024]{1,0:T(8,128)(2,1)S(1)} %bitcast.1, bf16[32,8192]{1,0:T(8,128)(2,1)S(1)} %copy-done), custom_call_target="tpu_custom_call" | custom-call | tf_op jit(solution)/shard_map/pallas_call | solution.py:227
  47.9 5.9 %shard_map.29 = bf16[1024,8192]{1,0:T(8,128)(2,1)} custom-call(bf16[3,1024,2048]{2,1,0:T(8,128)(2,1)S(1)} %get-tuple-element.8.part_ref, bf16[256,8192]{1,0:T(8,128)(2,1)S(1)} %get-tuple-element.9.whole_ref, bf16[1024,256]{1,0:T(8,128)(2,1)S(1)} %get-tuple-element.10.s_ref), custom_call_target="tpu_custom_call" | custom-call | tf_op jit(solution)/shard_map/pallas_call | solution.py:248
Async XLA Ops:
  0.0 1.0 %copy-start = (bf16[32,8192]{1,0:T(8,128)(2,1)S(1)}, bf16[32,8192]{1,0:T(8,128)(2,1)}, u32[]{:S(2)}) copy-start(bf16[32,8192]{1,0:T(8,128)(2,1)} %it_ref.1) | copy-start | bytes 1572868
  1.0 0.9 %copy-start.1 = (bf16[1024,64]{0,1:T(8,128)(2,1)S(1)}, bf16[1024,64]{0,1:T(8,128)(2,1)}, u32[]{:S(2)}) copy-start(bf16[1024,64]{0,1:T(8,128)(2,1)} %param.2) | copy-start | bytes 393220

commit v4 on v3

--- a/solution.py
+++ b/solution.py
@@ -243,7 +243,7 @@
             dma((3,)),
             dma((2,)),
         ],
-        compiler_params=pltpu.CompilerParams(collective_id=0, has_side_effects=True, vmem_limit_bytes=16 << 20),
+        compiler_params=pltpu.CompilerParams(collective_id=0, has_side_effects=True, vmem_limit_bytes=40 << 20),
     )(s_rows.T, iterate)
     return pl.pallas_call(
         write_kernel,

time: 54 us -> 52 us (0.963)
  local copies, waits for them, and re-layouts: 1.94 us -> 0 us
    unnamed x4 -> x0, local copies, waits for them, and re-layouts: 1.94 us -> none
where the time goes in v4:
time: 52 us; the launch traced here: 51.8 us
  Pallas kernels  51.8 us (100%)
    pallas_call x1, Pallas kernels, gathered(): pl.pallas_call(gather_kernel, out_shape=(pltpu.VMEM((CHUNKS - HOLD, rows,...  46 us
    pallas_call x1, Pallas kernels, gathered(): pl.pallas_call(write_kernel, in_specs=[vmem] * 3, out_specs=pl.BlockSpec(...  5.88 us

profile of v4, /device:TPU:0, one launch (start us, length us, event | category | flops | bytes accessed | tf_op | source)
XLA Modules:
  0.0 51.8 jit_solution(15174206340519201828)
XLA Ops:
  0.0 46.0 %shard_map.28 = (bf16[3,1024,2048]{2,1,0:T(8,128)(2,1)S(1)}, bf16[256,8192]{1,0:T(8,128)(2,1)S(1)}, bf16[1024,256]{1,0:T(8,128)(2,1)S(1)}) custom-call(bf16[64,1024]{1,0:T(8,128)(2,1)} %bitcast.1, bf16[32,8192]{1,0:T(8,128)(2,1)} %it_ref.1), custom_call_target="tpu_custom_call" | custom-call | tf_op jit(solution)/shard_map/pallas_call | solution.py:227
  46.0 5.9 %shard_map.29 = bf16[1024,8192]{1,0:T(8,128)(2,1)} custom-call(bf16[3,1024,2048]{2,1,0:T(8,128)(2,1)S(1)} %get-tuple-element.8.part_ref, bf16[256,8192]{1,0:T(8,128)(2,1)S(1)} %get-tuple-element.9.whole_ref, bf16[1024,256]{1,0:T(8,128)(2,1)S(1)} %get-tuple-element.10.s_ref), custom_call_target="tpu_custom_call" | custom-call | tf_op jit(solution)/shard_map/pallas_call | solution.py:248
